TPU v7x, 32 devices: a whole 2x2x4 slice. The times are simulated.
32 devices in a mesh: dp: 4 (over x, core), sp: 8 (over z, y).
Axes of the slice: x: 2, y: 2, z: 4, core: 2. Of those that a mesh axis runs over, the one named last changes fastest.
Arguments:
- frames_in: bfloat16 [2048, 64, 256], P(('dp', 'sp')), may hold values from -6 to 6
- spatial_weight: bfloat16 [3, 3, 256, 256], replicated, may hold values from -0.125 to 0.125
- temporal_weight: bfloat16 [3, 256, 256], replicated, may hold values from -0.21875 to 0.21875
- cotangent: bfloat16 [2048, 64, 256], P(('dp', 'sp')), may hold values from -6 to 6
Outputs:
- block_out: bfloat16 [2048, 64, 256], P(('dp', 'sp'))
- grad_input: bfloat16 [2048, 64, 256], P(('dp', 'sp'))
- grad_spatial: float32 [3, 3, 256, 256], replicated
- grad_temporal: float32 [3, 256, 256], replicated
All inputs are finite; a program needn't handle non-finite values.
Results may differ from a plain program's by a relative error of at most 0.0049.
Values may be sent and summed in bfloat16 or wider, within the bound.
A program may use at most 128 MiB of HBM per device.

v0:
```python
import math
import jax
import jax.numpy as jnp
from jax import lax
from jax.sharding import PartitionSpec as P

H = 64
FRAMES = 4


def contract_rows(left, right):
    return lax.dot_general(
        left, right, (((0,), (0,)), ((), ())), preferred_element_type=jnp.float32
    )


def times_transpose(left, weight):
    return lax.dot_general(
        left, weight, (((1,), (1,)), ((), ())), preferred_element_type=jnp.float32
    )


def local(frames_in, spatial_weight, temporal_weight, cotangent):
    slab_rows, width_cells, channels = frames_in.shape
    sp_count = lax.axis_size("sp")

    def padded_rows(values):
        return jnp.pad(values, ((1, 1), (1, 1), (0, 0)))

    def flatten_rows(values):
        return values.reshape(-1, channels)

    padded_in = padded_rows(frames_in)
    pre = jnp.zeros((slab_rows * width_cells, channels), jnp.float32)
    for tap_row in range(3):
        for tap_col in range(3):
            window = flatten_rows(
                padded_in[tap_row : tap_row + slab_rows, tap_col : tap_col + width_cells]
            )
            pre = pre + jnp.dot(
                window, spatial_weight[tap_row, tap_col], preferred_element_type=jnp.float32
            )
    act = jax.nn.silu(pre).astype(jnp.bfloat16).reshape(slab_rows, width_cells, channels)

    def to_frames(values):
        return lax.all_to_all(values, "sp", split_axis=0, concat_axis=1, tiled=True)

    moved_act, moved_cot = (
        lax.all_to_all(act, "sp", split_axis=1, concat_axis=0, tiled=True),
        lax.all_to_all(cotangent, "sp", split_axis=1, concat_axis=0, tiled=True),
    )
    group_rows = slab_rows * sp_count
    stripe = width_cells // sp_count
    groups = group_rows // (FRAMES * H)
    act_clips = moved_act.reshape(groups, FRAMES, H * stripe, channels)
    cot_clips = moved_cot.reshape(groups, FRAMES, H * stripe, channels)
    act_padded = jnp.pad(act_clips, ((0, 0), (2, 0), (0, 0), (0, 0)))
    cot_padded = jnp.pad(cot_clips, ((0, 0), (0, 2), (0, 0), (0, 0)))
    temporal_sum = jnp.zeros(act_clips.shape, jnp.float32)
    act_grad_sum = jnp.zeros(act_clips.shape, jnp.float32)
    temporal_terms = []
    for tap_step in range(3):
        earlier = act_padded[:, 2 - tap_step : 2 - tap_step + FRAMES]
        temporal_sum = temporal_sum + jnp.einsum(
            "gfpc,cd->gfpd", earlier, temporal_weight[tap_step], preferred_element_type=jnp.float32
        )
        temporal_terms.append(
            jnp.einsum("gfpc,gfpd->cd", earlier, cot_clips, preferred_element_type=jnp.float32)
        )
        later = cot_padded[:, tap_step : tap_step + FRAMES]
        act_grad_sum = act_grad_sum + jnp.einsum(
            "gfpd,cd->gfpc", later, temporal_weight[tap_step], preferred_element_type=jnp.float32
        )
    temporal_out = to_frames(
        temporal_sum.astype(jnp.bfloat16).reshape(group_rows, stripe, channels)
    )
    grad_act = to_frames(act_grad_sum.astype(jnp.bfloat16).reshape(group_rows, stripe, channels))
    grad_temporal = jnp.stack(temporal_terms)
    grad_scale = 1.0 / math.sqrt(slab_rows * sp_count * lax.axis_size("dp") * width_cells)
    block_out = (frames_in.astype(jnp.float32) + temporal_out.astype(jnp.float32)).astype(
        jnp.bfloat16
    )
    sigma = jax.nn.sigmoid(pre)
    grad_pre = (
        flatten_rows(grad_act).astype(jnp.float32) * (sigma * (1.0 + pre * (1.0 - sigma)))
    ).astype(jnp.bfloat16)
    grad_padded = padded_rows(grad_pre.reshape(slab_rows, width_cells, channels))
    spatial_terms = []
    grad_in = flatten_rows(cotangent).astype(jnp.float32)
    for tap_row in range(3):
        for tap_col in range(3):
            window = flatten_rows(
                padded_in[tap_row : tap_row + slab_rows, tap_col : tap_col + width_cells]
            )
            spatial_terms.append(contract_rows(window, grad_pre))
            back_window = flatten_rows(
                grad_padded[
                    2 - tap_row : 2 - tap_row + slab_rows, 2 - tap_col : 2 - tap_col + width_cells
                ]
            )
            grad_in = grad_in + times_transpose(back_window, spatial_weight[tap_row, tap_col])
    grad_spatial = jnp.stack(spatial_terms).reshape(3, 3, channels, channels)
    grad_spatial, grad_temporal = lax.psum((grad_spatial, grad_temporal), ("dp", "sp"))
    grad_input = grad_in.astype(jnp.bfloat16).reshape(slab_rows, width_cells, channels)
    return (block_out, grad_input, grad_spatial * grad_scale, grad_temporal * grad_scale)


def solution(mesh):
    placed = (P(("dp", "sp"), None, None), P(), P(), P(("dp", "sp"), None, None))
    return jax.shard_map(
        local,
        mesh=mesh,
        in_specs=placed,
        out_specs=(P(("dp", "sp"), None, None), P(("dp", "sp"), None, None), P(), P()),
        check_vma=False,
    )
```

profile of v0, /device:TPU:0, one launch (start us, length us, event | category | flops | bytes accessed | tf_op | source)
XLA Modules:
  0.0 385.7 jit_solution(17746489602125472998)
XLA Ops:
  7.2 4.1 %copy.32 = bf16[64,64,256]{2,0,1:T(8,128)(2,1)} copy(bf16[64,64,256]{2,1,0:T(8,128)(2,1)} %param.7) | data formatting | bytes 4194304 | tf_op args[3]
  11.3 7.4 %all-to-all-start.2 = ((bf16[64,64,256]{2,0,1:T(8,128)(2,1)}), bf16[64,64,256]{2,0,1:T(8,128)(2,1)}, u32[]{:S(2)}, u32[]{:S(2)}) async-start(bf16[64,64,256]{2,0,1:T(8,128)(2,1)} %copy.32), calls=%async_computation.2 | async-start | bytes 4194304 | tf_op jit(solution)/shard_map/all_to_all | solution.py:50
  18.7 9.8 %pad_slice_fusion.10 = (bf16[64,64,256]{2,1,0:T(8,128)(2,1)}, bf16[64,64,256]{2,1,0:T(8,128)(2,1)}, bf16[64,64,256]{2,1,0:T(8,128)(2,1)}, bf16[64,64,256]{2,1,0:...) fusion(bf16[64,64,256]{2,1,0:T(8,128)(2,1)S(1)} %copy-done.3), kind=kLoop, calls=%fused_computation.46 | loop fusion | bytes 18874368 | tf_op jit(solution)/shard_map/slice | solution.py:38
  28.4 38.6 %all-to-all-done.2 = bf16[64,64,256]{2,0,1:T(8,128)(2,1)} async-done(((bf16[64,64,256]{2,0,1:T(8,128)(2,1)}), bf16[64,64,256]{2,0,1:T(8,128)(2,1)}, u32[]{:S(2)}, u32[]{:S(2)}) %all-to-all-start.2) | async-done | bytes 2097184 | tf_op jit(solution)/shard_map/all_to_all | solution.py:50
  67.0 2.9 copy.33
  71.4 2.1 add_convert_fusion
  73.5 4.8 %all-to-all-start.3 = ((bf16[512,8,256]{2,1,0:T(8,128)(2,1)}), bf16[512,8,256]{2,1,0:T(8,128)(2,1)}, u32[]{:S(2)}, u32[]{:S(2)}) async-start(bf16[512,8,256]{2,1,0:T(8,128)(2,1)} %bitcast.239), calls=%async_computation.3 | async-start | bytes 4194304 | tf_op jit(solution)/shard_map/all_to_all | solution.py:46
  78.3 2.4 fusion.63
  89.4 2.7 convolution_add_fusion.10
  92.1 34.0 %all-to-all-done.3 = bf16[512,8,256]{2,1,0:T(8,128)(2,1)} async-done(((bf16[512,8,256]{2,1,0:T(8,128)(2,1)}), bf16[512,8,256]{2,1,0:T(8,128)(2,1)}, u32[]{:S(2)}, u32[]{:S(2)}) %all-to-all-start.3) | async-done | bytes 2097184 | tf_op jit(solution)/shard_map/all_to_all | solution.py:46
  126.1 2.0 convert_bitcast_fusion
  128.7 1.6 copy-done.23
  130.9 3.5 fusion.2
  134.4 2.5 copy.29
  137.0 4.9 %all-to-all-start = ((bf16[64,64,256]{2,0,1:T(8,128)(2,1)}), bf16[64,64,256]{2,0,1:T(8,128)(2,1)}, u32[]{:S(2)}, u32[]{:S(2)}) async-start(bf16[64,64,256]{2,0,1:T(8,128)(2,1)} %copy.29), calls=%async_computation | async-start | bytes 4194304 | tf_op jit(solution)/shard_map/all_to_all | solution.py:49
  141.9 3.1 fusion.35
  149.3 1.0 fusion.31
  156.4 1.4 copy-done.24
  157.8 10.4 %pad_slice_fusion.2 = (bf16[64,64,256]{2,1,0:T(8,128)(2,1)}, bf16[64,64,256]{2,1,0:T(8,128)(2,1)S(1)}, bf16[64,64,256]{2,1,0:T(8,128)(2,1)S(1)}, bf16[64,64,256]...) fusion(bf16[64,64,256]{2,1,0:T(8,128)(2,1)S(1)} %bitcast.256), kind=kLoop, calls=%fused_computation.38 | loop fusion | bytes 18874368 | tf_op jit(solution)/shard_map/slice | solution.py:97
  171.3 2.8 convolution_add_fusion.4
  174.1 15.5 %all-to-all-done = bf16[64,64,256]{2,0,1:T(8,128)(2,1)} async-done(((bf16[64,64,256]{2,0,1:T(8,128)(2,1)}), bf16[64,64,256]{2,0,1:T(8,128)(2,1)}, u32[]{:S(2)}, u32[]{:S(2)}) %all-to-all-start) | async-done | bytes 2097184 | tf_op jit(solution)/shard_map/all_to_all | solution.py:49
  189.6 3.0 copy.30
  195.1 2.0 add_convert_fusion.1
  197.1 4.4 %all-to-all-start.1 = ((bf16[512,8,256]{2,1,0:T(8,128)(2,1)}), bf16[512,8,256]{2,1,0:T(8,128)(2,1)}, u32[]{:S(2)}, u32[]{:S(2)}) async-start(bf16[512,8,256]{2,1,0:T(8,128)(2,1)} %bitcast.238), calls=%async_computation.1 | async-start | bytes 4194304 | tf_op jit(solution)/shard_map/all_to_all | solution.py:46
  202.0 1.3 copy-done.2
  204.8 0.9 pad_maximum_fusion
  205.8 3.7 convolution_add_fusion.3
  212.7 2.1 fusion
  214.8 154.8 %all-reduce.7.cloned.1.call-done = (f32[3,3,256,256]{3,2,1,0:T(8,128)}, f32[3,256,256]{2,1,0:T(8,128)}) async-done(((f32[3,3,256,256]{3,2,1,0:T(8,128)}, f32[3,256,256]{2,1,0:T(8,128)}), (f32[3,3,256,256]{3,2,1,0:T(8,128)}, f32[3,256,256]{2,1,0:T(8,128)})) %all-reduce.7.cloned.1.call-update) | async-done | bytes 3145744 | tf_op jit(solution)/shard_map/psum | solution.py:103
  369.6 2.1 broadcast_multiply_fusion.1
  371.6 3.4 broadcast_multiply_fusion
  375.1 3.6 fusion.1
  (86 shorter events, 32.4 us)
Async XLA Ops:
  11.2 7.4 %copy-start.3 = (bf16[64,64,256]{2,1,0:T(8,128)(2,1)S(1)}, bf16[64,64,256]{2,1,0:T(8,128)(2,1)}, u32[]{:S(2)}) copy-start(bf16[64,64,256]{2,1,0:T(8,128)(2,1)} %param.4) | copy-start | bytes 6291460
  11.3 55.8 %all-to-all-start.2 = ((bf16[64,64,256]{2,0,1:T(8,128)(2,1)}), bf16[64,64,256]{2,0,1:T(8,128)(2,1)}, u32[]{:S(2)}, u32[]{:S(2)}) async-start(bf16[64,64,256]{2,0,1:T(8,128)(2,1)} %copy.32), calls=%async_computation.2 | async-start | bytes 4194304 | tf_op jit(solution)/shard_map/all_to_all | solution.py:50
  67.0 2.9 copy-start.27
  69.9 1.5 copy-start
  73.5 4.8 %copy-start.22 = (bf16[3,3,256,256]{3,2,1,0:T(8,128)(2,1)S(1)}, bf16[3,3,256,256]{3,2,1,0:T(8,128)(2,1)}, u32[]{:S(2)}) copy-start(bf16[3,3,256,256]{3,2,1,0:T(8,128)(2,1)} %param.5) | copy-start | bytes 3538948
  73.5 52.6 %all-to-all-start.3 = ((bf16[512,8,256]{2,1,0:T(8,128)(2,1)}), bf16[512,8,256]{2,1,0:T(8,128)(2,1)}, u32[]{:S(2)}, u32[]{:S(2)}) async-start(bf16[512,8,256]{2,1,0:T(8,128)(2,1)} %bitcast.239), calls=%async_computation.3 | async-start | bytes 4194304 | tf_op jit(solution)/shard_map/all_to_all | solution.py:46
  78.3 2.5 copy-start.19
  80.8 1.6 copy-start.16
  82.4 1.6 copy-start.13
  84.7 1.6 copy-start.10
  86.3 1.6 copy-start.8
  87.8 1.6 copy-start.6
  128.1 2.2 copy-start.23
  128.1 2.9 copy-start.25
  137.0 52.7 %all-to-all-start = ((bf16[64,64,256]{2,0,1:T(8,128)(2,1)}), bf16[64,64,256]{2,0,1:T(8,128)(2,1)}, u32[]{:S(2)}, u32[]{:S(2)}) async-start(bf16[64,64,256]{2,0,1:T(8,128)(2,1)} %copy.29), calls=%async_computation | async-start | bytes 4194304 | tf_op jit(solution)/shard_map/all_to_all | solution.py:49
  141.9 3.1 copy-start.20
  141.9 3.5 copy-start.21
  145.3 1.6 copy-start.17
  146.9 1.6 copy-start.14
  149.3 1.6 copy-start.11
  150.9 1.6 copy-start.9
  152.5 1.6 copy-start.7
  154.1 1.6 copy-start.26
  157.8 10.5 %copy-start.5 = (bf16[64,64,256]{2,1,0:T(8,128)(2,1)S(1)}, bf16[64,64,256]{2,1,0:T(8,128)(2,1)}, u32[]{:S(2)}) copy-start(bf16[64,64,256]{2,1,0:T(8,128)(2,1)} %param.7) | copy-start | bytes 6291460
  189.6 3.0 copy-start.1
  197.1 178.0 %all-to-all-start.1 = ((bf16[512,8,256]{2,1,0:T(8,128)(2,1)}), bf16[512,8,256]{2,1,0:T(8,128)(2,1)}, u32[]{:S(2)}, u32[]{:S(2)}) async-start(bf16[512,8,256]{2,1,0:T(8,128)(2,1)} %bitcast.238), calls=%async_computation.1 | async-start | bytes 4194304 | tf_op jit(solution)/shard_map/all_to_all | solution.py:46
  201.5 168.1 %all-reduce.7.cloned.1.call-start = ((), (), s32[]{:S(2)}) async-start(), calls=%async_computation.4 | async-start | bytes 6291456 | tf_op jit(solution)/shard_map/psum | solution.py:103
  201.7 1.6 copy-start.2
  205.8 3.7 copy-start.18
  209.5 1.6 copy-start.15
  211.1 1.6 copy-start.12
  371.6 3.4 copy-start.4
  (2 other events, 2.4 us)
Sparse Core Ops, SparseCore 0:
  208.5 160.9 all-reduce.6
where the time goes:
time: 393 us; the launch traced here: 386 us
  waiting for transfers between devices  243 us (62%)
  local copies, waits for them, and re-layouts  49.7 us (13%)
  matrix products  44.8 us (11%)
  starting transfers between devices  21.7 us (6%)
  between operations  14.7 us (4%)
  other arithmetic  12 us (3%)
    psum x1, waiting for transfers between devices, local(): lax.psum((grad_spatial, grad_temporal), ('dp', 'sp'))  155 us
    all_to_all x1, waiting for transfers between devices, local(): lax.all_to_all(cotangent, 'sp', split_axis=1, concat_axis=0, tiled=True)  38.6 us
    all_to_all x2, waiting for transfers between devices, to_frames(): return lax.all_to_all(values, 'sp', split_axis=0, concat_axis=1, tiled=True)  34 us
    unnamed x59, local copies, waits for them, and re-layouts  20.2 us
    all_to_all x1, waiting for transfers between devices, local(): lax.all_to_all(act, 'sp', split_axis=1, concat_axis=0, tiled=True)  15.5 us
    dot_general x9, matrix products, times_transpose(): lax.dot_general(left, weight, (((1,), (1,)), ((), ())), preferred_element...  13.1 us
    dot_general x9, matrix products, local(): jnp.dot(window, spatial_weight[tap_row, tap_col], preferred_element_type=...  13 us
    slice x1, local copies, waits for them, and re-layouts, local(): grad_padded[2 - tap_row:2 - tap_row + slab_rows, 2 - tap_col:2 - tap_col...  10.4 us
  transfers between devices with their start and end apart: 5, of which 4 were waited for; matrix products, arithmetic and copies ran while one was open for 16% of the time, Pallas kernels for 0%

commit v1 on v0

--- a/solution.py
+++ b/solution.py
@@ -47,7 +47,12 @@
 
     moved_act, moved_cot = (
         lax.all_to_all(act, "sp", split_axis=1, concat_axis=0, tiled=True),
-        lax.all_to_all(cotangent, "sp", split_axis=1, concat_axis=0, tiled=True),
+        jnp.concatenate(
+            lax.all_to_all(
+                jnp.stack(jnp.split(cotangent, lax.axis_size("sp"), axis=1)), "sp", 0, 0
+            ),
+            axis=0,
+        ),
     )
     group_rows = slab_rows * sp_count
     stripe = width_cells // sp_count

time: 393 us -> 392 us (level); the launches traced: 386 us -> 391 us
  local copies, waits for them, and re-layouts: 49.7 us -> 62.1 us
  waiting for transfers between devices: 243 us -> 239 us
    unnamed x59 -> x69, local copies, waits for them, and re-layouts: 20.2 us -> 30.4 us
where the time goes in v1:
time: 392 us; the launch traced here: 391 us
  waiting for transfers between devices  239 us (61%)
  local copies, waits for them, and re-layouts  62.1 us (16%)
  matrix products  42.3 us (11%)
  starting transfers between devices  21.4 us (5%)
  between operations  14.4 us (4%)
  other arithmetic  11.9 us (3%)
    psum x1, waiting for transfers between devices, local(): lax.psum((grad_spatial, grad_temporal), ('dp', 'sp'))  154 us
    all_to_all x1, waiting for transfers between devices, local(): lax.all_to_all(jnp.stack(jnp.split(cotangent, lax.axis_size('sp'), axis=1...  35 us
    all_to_all x2, waiting for transfers between devices, to_frames(): return lax.all_to_all(values, 'sp', split_axis=0, concat_axis=1, tiled=True)  33.9 us
    unnamed x69, local copies, waits for them, and re-layouts  30.4 us
    all_to_all x1, waiting for transfers between devices, local(): lax.all_to_all(act, 'sp', split_axis=1, concat_axis=0, tiled=True)  15.6 us
    slice x1, local copies, waits for them, and re-layouts, local(): padded_in[tap_row:tap_row + slab_rows, tap_col:tap_col + width_cells]  13.2 us
    dot_general x9, matrix products, times_transpose(): lax.dot_general(left, weight, (((1,), (1,)), ((), ())), preferred_element...  12.4 us
    dot_general x9, matrix products, local(): jnp.dot(window, spatial_weight[tap_row, tap_col], preferred_element_type=...  11.2 us
  transfers between devices with their start and end apart: 5, of which 4 were waited for; matrix products, arithmetic and copies ran while one was open for 16% of the time, Pallas kernels for 0%

profile of v1, /device:TPU:0, one launch (start us, length us, event | category | flops | bytes accessed | tf_op | source)
XLA Modules:
  0.0 390.6 jit_solution(12950314654318129451)
XLA Ops:
  7.2 1.7 bitcast_dynamic-update-slice_fusion.7
  8.8 1.7 bitcast_dynamic-update-slice_fusion.6
  10.5 1.7 bitcast_dynamic-update-slice_fusion.5
  12.2 1.7 bitcast_dynamic-update-slice_fusion.4
  13.8 1.7 bitcast_dynamic-update-slice_fusion.3
  15.5 1.7 bitcast_dynamic-update-slice_fusion.2
  17.2 1.7 bitcast_dynamic-update-slice_fusion.1
  18.8 1.7 bitcast_dynamic-update-slice_fusion
  20.5 7.3 %all-to-all-start.2 = ((bf16[8,64,8,256]{3,2,1,0:T(8,128)(2,1)}), bf16[8,64,8,256]{3,2,1,0:T(8,128)(2,1)S(1)}, u32[]{:S(2)}, u32[]{:S(2)}) async-start(bf16[8,64,8,256]{3,2,1,0:T(8,128)(2,1)} %bitcast_dynamic-update-slice_fusion), calls=%async_computation.2 | async-start | bytes 4194304 | tf_op jit(solution)/shard_map/all_to_all | solution.py:51
  27.8 13.2 %pad_slice_fusion.10 = (bf16[64,64,256]{2,1,0:T(8,128)(2,1)}, bf16[64,64,256]{2,1,0:T(8,128)(2,1)}, bf16[64,64,256]{2,1,0:T(8,128)(2,1)}, bf16[64,64,256]{2,1,0:...) fusion(bf16[64,64,256]{2,1,0:T(8,128)(2,1)} %param.4), kind=kLoop, calls=%fused_computation.46 | loop fusion | bytes 18874368 | tf_op jit(solution)/shard_map/slice | solution.py:38
  41.1 35.0 %all-to-all-done.2 = bf16[8,64,8,256]{3,2,1,0:T(8,128)(2,1)S(1)} async-done(((bf16[8,64,8,256]{3,2,1,0:T(8,128)(2,1)}), bf16[8,64,8,256]{3,2,1,0:T(8,128)(2,1)S(1)}, u32[]{:S(2)}, u32[]{:S(2)}) %all-to-all-start.2) | async-done | bytes 2097184 | tf_op jit(solution)/shard_map/all_to_all | solution.py:51
  77.5 2.1 add_convert_fusion
  79.6 4.8 %all-to-all-start.3 = ((bf16[512,8,256]{2,1,0:T(8,128)(2,1)}), bf16[512,8,256]{2,1,0:T(8,128)(2,1)}, u32[]{:S(2)}, u32[]{:S(2)}) async-start(bf16[512,8,256]{2,1,0:T(8,128)(2,1)} %bitcast.252), calls=%async_computation.3 | async-start | bytes 4194304 | tf_op jit(solution)/shard_map/all_to_all | solution.py:46
  95.6 2.7 convolution_add_fusion.10
  98.3 33.9 %all-to-all-done.3 = bf16[512,8,256]{2,1,0:T(8,128)(2,1)} async-done(((bf16[512,8,256]{2,1,0:T(8,128)(2,1)}), bf16[512,8,256]{2,1,0:T(8,128)(2,1)}, u32[]{:S(2)}, u32[]{:S(2)}) %all-to-all-start.3) | async-done | bytes 2097184 | tf_op jit(solution)/shard_map/all_to_all | solution.py:46
  132.1 2.0 convert_bitcast_fusion
  137.0 3.5 fusion.2
  140.4 2.5 copy.27
  143.0 4.6 %all-to-all-start = ((bf16[64,64,256]{2,0,1:T(8,128)(2,1)}), bf16[64,64,256]{2,0,1:T(8,128)(2,1)}, u32[]{:S(2)}, u32[]{:S(2)}) async-start(bf16[64,64,256]{2,0,1:T(8,128)(2,1)} %copy.27), calls=%async_computation | async-start | bytes 4194304 | tf_op jit(solution)/shard_map/all_to_all | solution.py:49
  147.6 3.1 fusion.35
  163.5 10.3 %pad_slice_fusion.2 = (bf16[64,64,256]{2,1,0:T(8,128)(2,1)}, bf16[64,64,256]{2,1,0:T(8,128)(2,1)S(1)}, bf16[64,64,256]{2,1,0:T(8,128)(2,1)S(1)}, bf16[64,64,256]...) fusion(bf16[64,64,256]{2,1,0:T(8,128)(2,1)S(1)} %bitcast.269), kind=kLoop, calls=%fused_computation.38 | loop fusion | bytes 18874368 | tf_op jit(solution)/shard_map/slice | solution.py:102
  176.8 2.8 convolution_add_fusion.4
  179.6 15.6 %all-to-all-done = bf16[64,64,256]{2,0,1:T(8,128)(2,1)} async-done(((bf16[64,64,256]{2,0,1:T(8,128)(2,1)}), bf16[64,64,256]{2,0,1:T(8,128)(2,1)}, u32[]{:S(2)}, u32[]{:S(2)}) %all-to-all-start) | async-done | bytes 2097184 | tf_op jit(solution)/shard_map/all_to_all | solution.py:49
  195.2 3.0 copy.28
  200.6 2.0 add_convert_fusion.1
  202.6 4.4 %all-to-all-start.1 = ((bf16[512,8,256]{2,1,0:T(8,128)(2,1)}), bf16[512,8,256]{2,1,0:T(8,128)(2,1)}, u32[]{:S(2)}, u32[]{:S(2)}) async-start(bf16[512,8,256]{2,1,0:T(8,128)(2,1)} %bitcast.251), calls=%async_computation.1 | async-start | bytes 4194304 | tf_op jit(solution)/shard_map/all_to_all | solution.py:46
  212.3 3.1 convolution_add_fusion.3
  218.6 2.1 fusion
  220.6 154.1 %all-reduce.7.cloned.1.call-done = (f32[3,3,256,256]{3,2,1,0:T(8,128)}, f32[3,256,256]{2,1,0:T(8,128)}) async-done(((f32[3,3,256,256]{3,2,1,0:T(8,128)}, f32[3,256,256]{2,1,0:T(8,128)}), (f32[3,3,256,256]{3,2,1,0:T(8,128)}, f32[3,256,256]{2,1,0:T(8,128)})) %all-reduce.7.cloned.1.call-update) | async-done | bytes 3145744 | tf_op jit(solution)/shard_map/psum | solution.py:108
  374.8 2.1 broadcast_multiply_fusion.1
  376.9 3.4 broadcast_multiply_fusion
  380.3 3.5 fusion.1
  (96 shorter events, 41.9 us)
Async XLA Ops:
  20.5 55.5 %all-to-all-start.2 = ((bf16[8,64,8,256]{3,2,1,0:T(8,128)(2,1)}), bf16[8,64,8,256]{3,2,1,0:T(8,128)(2,1)S(1)}, u32[]{:S(2)}, u32[]{:S(2)}) async-start(bf16[8,64,8,256]{3,2,1,0:T(8,128)(2,1)} %bitcast_dynamic-update-slice_fusion), calls=%async_computation.2 | async-start | bytes 4194304 | tf_op jit(solution)/shard_map/all_to_all | solution.py:51
  27.8 48.2 %copy-start.29 = (bf16[3,256,256]{2,1,0:T(8,128)(2,1)S(1)}, bf16[3,256,256]{2,1,0:T(8,128)(2,1)}, u32[]{:S(2)}) copy-start(bf16[3,256,256]{2,1,0:T(8,128)(2,1)} %param.6) | copy-start | bytes 1179652
  79.6 4.8 %copy-start.6 = (bf16[64,64,256]{2,1,0:T(8,128)(2,1)S(1)}, bf16[64,64,256]{2,1,0:T(8,128)(2,1)}, u32[]{:S(2)}) copy-start(bf16[64,64,256]{2,1,0:T(8,128)(2,1)} %get-tuple-element.25) | copy-start | bytes 6291460
  79.6 4.8 %copy-start.24 = (bf16[3,3,256,256]{3,2,1,0:T(8,128)(2,1)S(1)}, bf16[3,3,256,256]{3,2,1,0:T(8,128)(2,1)}, u32[]{:S(2)}) copy-start(bf16[3,3,256,256]{3,2,1,0:T(8,128)(2,1)} %param.5) | copy-start | bytes 3538948
  79.6 52.5 %all-to-all-start.3 = ((bf16[512,8,256]{2,1,0:T(8,128)(2,1)}), bf16[512,8,256]{2,1,0:T(8,128)(2,1)}, u32[]{:S(2)}, u32[]{:S(2)}) async-start(bf16[512,8,256]{2,1,0:T(8,128)(2,1)} %bitcast.252), calls=%async_computation.3 | async-start | bytes 4194304 | tf_op jit(solution)/shard_map/all_to_all | solution.py:46
  84.4 1.6 copy-start.21
  86.0 1.6 copy-start.18
  87.6 1.6 copy-start.15
  89.2 1.6 copy-start.3
  90.8 1.6 copy-start.11
  92.4 1.6 copy-start.9
  94.0 1.6 copy-start.7
  134.1 2.2 copy-start.25
  134.1 2.9 copy-start.27
  143.0 52.2 %all-to-all-start = ((bf16[64,64,256]{2,0,1:T(8,128)(2,1)}), bf16[64,64,256]{2,0,1:T(8,128)(2,1)}, u32[]{:S(2)}, u32[]{:S(2)}) async-start(bf16[64,64,256]{2,0,1:T(8,128)(2,1)} %copy.27), calls=%async_computation | async-start | bytes 4194304 | tf_op jit(solution)/shard_map/all_to_all | solution.py:49
  147.6 3.1 copy-start.22
  147.6 3.5 copy-start.23
  151.0 1.6 copy-start.19
  152.6 1.6 copy-start.16
  155.0 1.6 copy-start.12
  156.6 1.6 copy-start.10
  158.2 1.6 copy-start.8
  159.8 1.6 copy-start.28
  163.5 10.3 %copy-start.5 = (bf16[64,64,256]{2,1,0:T(8,128)(2,1)S(1)}, bf16[64,64,256]{2,1,0:T(8,128)(2,1)}, u32[]{:S(2)}) copy-start(bf16[64,64,256]{2,1,0:T(8,128)(2,1)} %param.7) | copy-start | bytes 6291460
  195.2 3.0 copy-start.1
  202.6 177.7 %all-to-all-start.1 = ((bf16[512,8,256]{2,1,0:T(8,128)(2,1)}), bf16[512,8,256]{2,1,0:T(8,128)(2,1)}, u32[]{:S(2)}, u32[]{:S(2)}) async-start(bf16[512,8,256]{2,1,0:T(8,128)(2,1)} %bitcast.251), calls=%async_computation.1 | async-start | bytes 4194304 | tf_op jit(solution)/shard_map/all_to_all | solution.py:46
  207.0 167.8 %all-reduce.7.cloned.1.call-start = ((), (), s32[]{:S(2)}) async-start(), calls=%async_computation.4 | async-start | bytes 6291456 | tf_op jit(solution)/shard_map/psum | solution.py:108
  207.3 1.6 copy-start.2
  210.4 1.9 copy-start.20
  212.3 3.1 copy-start.17
  215.4 1.6 copy-start.14
  376.9 3.4 copy-start.4
  (4 other events, 5.5 us)
Sparse Core Ops, SparseCore 0:
  214.0 160.7 all-reduce.6
